TPU v7x, 1024 devices: a whole 4x4x32 slice. The times are simulated.
1024 devices in a mesh: prow: 16 (over z_hi, y), pcol: 64 (over x, z_lo, core).
Axes of the slice: x: 4, y: 4, z: 32 (z_hi: 4, z_lo: 8; z = z_hi * 8 + z_lo), core: 2. Of those that a mesh axis runs over, the one named last changes fastest.
Arguments:
- matrix: float32 [8192, 8192], P('prow', 'pcol'), may hold values from -6 to 6
- panel: float32 [8192, 1024], P(('prow', 'pcol')), as said below
- pivots: int32 [1024], replicated, may hold values from 0 to 8191, as said below
Outputs:
- trailing: float32 [8192, 8192], P('prow', 'pcol')
Inputs may be any that keep to these rules, and one draw needn't show every extreme that they name: pivots[i] is either i itself or a row at or beyond 1024; the rows at or beyond 1024 that are named are all different; at most 44 of them lie in the rows of one index of prow, and some index of prow holds exactly 44. `panel`: the top 1024 rows are unit lower triangular.
All inputs are finite; a program needn't handle non-finite values.
Results may differ from a plain program's by a relative error of at most 0.000061.
Values sent between devices are 32-bit elements; how exact they have to be, the bound alone decides.
A program may use at most 32 MiB of HBM per device.

v0:
```python
import jax
import jax.numpy as jnp
from jax import lax
from jax.sharding import PartitionSpec as P


def spread(block, axis, holder):
    block = jnp.where(lax.axis_index(axis) == holder, block, jnp.zeros_like(block))
    return lax.psum(block, axis)


def per_device(matrix, panel, pivots):
    rows, cols = matrix.shape
    block = pivots.shape[0]
    first = lax.axis_index("prow") * rows
    local_pivot = pivots - first
    owned = (local_pivot >= 0) & (local_pivot < rows)
    picked = jnp.take(matrix, jnp.clip(local_pivot, 0, rows - 1), axis=0)
    picked = jnp.where(owned[:, None], picked, 0.0)
    panel_block = lax.all_gather(panel, "pcol", axis=0, tiled=True)
    pivot_block = lax.psum(picked, "prow")
    solved = jnp.dot(
        panel_block,
        pivot_block,
        precision=lax.Precision.HIGHEST,
        preferred_element_type=jnp.float32,
    )
    rows_here = first + jnp.arange(rows, dtype=jnp.int32)
    match = pivots[None, :] == rows_here[:, None]
    moved = jnp.any(match, axis=1) & (rows_here >= block)
    source = jnp.sum(jnp.where(match, jnp.arange(block, dtype=jnp.int32)[None, :], 0), axis=1)
    upper = jnp.zeros((block, cols), jnp.float32)
    top_old = jnp.zeros((block, cols), jnp.float32)
    for root in range(block // rows):
        piece_u, old_rows = (spread(solved, "prow", root), spread(matrix, "prow", root))
        upper = lax.dynamic_update_slice_in_dim(upper, piece_u, root * rows, 0)
        top_old = lax.dynamic_update_slice_in_dim(top_old, old_rows, root * rows, 0)
    replaced = jnp.take(top_old, source, axis=0)
    permuted = jnp.where(moved[:, None], replaced, matrix)
    lower = permuted - jnp.dot(
        panel_block, upper, precision=lax.Precision.HIGHEST, preferred_element_type=jnp.float32
    )
    return jnp.where((rows_here < block)[:, None], solved, lower)


def solution(mesh):
    placed = (P("prow", "pcol"), P(("prow", "pcol"), None), P())
    return jax.shard_map(
        per_device, mesh=mesh, in_specs=placed, out_specs=P("prow", "pcol"), check_vma=False
    )
```

profile of v0, /device:TPU:216, one launch (start us, length us, event | category | flops | bytes accessed | tf_op | source)
XLA Modules:
  0.0 678.0 jit_solution(4960964516710466911)
XLA Ops:
  7.4 0.0 all-reduce.4.cloned.1.call-start
  7.4 0.7 fusion.6
  8.1 0.7 compare_and_fusion.1
  8.8 0.0 copy-start
  8.8 3.8 gather_fusion
  12.6 1.1 select_select_fusion
  13.7 0.0 all-reduce.4.cloned.1.call-update
  13.8 0.0 all-gather.2.cloned.1.call-start
  13.8 0.5 all-gather.2.cloned.1.call-update
  14.3 0.0 all-reduce.6.cloned.1.call-start
  14.4 0.0 copy-done
  14.4 0.1 copy.16
  14.6 0.9 broadcast_select_fusion.3
  15.4 0.0 copy-start.3
  15.4 297.3 %all-reduce.4.cloned.1.call-done = f32[1024,128]{1,0:T(8,128)} async-done(((f32[1024,128]{1,0:T(8,128)}), f32[1024,128]{1,0:T(8,128)}) %all-reduce.4.cloned.1.call-update) | async-done | bytes 524304 | tf_op jit(solution)/shard_map/psum | solution.py:21
  312.7 0.0 all-gather.2.cloned.1.call-done
  312.7 5.0 broadcast_select_fusion.1
  317.7 0.0 all-reduce.6.cloned.1.call-update
  317.7 0.0 copy-done.3
  317.7 0.4 fusion
  318.2 0.4 compare_reduce_fusion
  318.6 345.2 %all-reduce.6.cloned.1.call-done = (f32[512,128]{0,1:T(8,128)}, f32[512,128]{0,1:T(8,128)}, f32[512,128]{0,1:T(8,128)}, f32[512,128]{0,1:T(8,128)}) async-done(((f32[512,128]{0,1:T(8,128)}, f32[512,128]{0,1:T(8,128)}, f32[512,128]{0,1:T(8,128)}, f32[512,128]{0,1:T(8,128)}), (f32[512,128]{0,1:T(8,128)}, f32[512,128]{0,1:T(8,128)}, f32[512,128]{0,1:T(8,128)}, ...) | async-done | bytes 1048592 | tf_op jit(solution)/shard_map/psum | solution.py:9
  663.7 1.1 pad_maximum_fusion
  664.8 0.0 copy-start.1
  664.8 0.2 copy.18
  665.0 0.0 copy-start.2
  665.0 1.0 gather_fusion.1
  666.1 0.1 copy.19
  666.2 0.2 copy-done.1
  666.4 0.0 copy-done.2
  666.4 3.3 fusion.2
  669.7 0.8 copy.21
  (5 shorter events, 0.0 us)
Async XLA Ops:
  7.4 305.4 %all-reduce.4.cloned.1.call-start = ((), (), s32[]{:S(2)}) async-start(), calls=%async_computation | async-start | bytes 1048576 | tf_op jit(solution)/shard_map/psum | solution.py:21
  8.8 5.6 copy-start
  13.8 299.0 %all-gather.2.cloned.1.call-start = ((), (), s32[]{:S(2)}) async-start(), calls=%async_computation.1 | async-start | bytes 2129920 | tf_op jit(solution)/shard_map/all_gather | solution.py:20
  14.3 649.4 %all-reduce.6.cloned.1.call-start = ((), (), s32[]{:S(2)}) async-start(), calls=%async_computation.2 | async-start | bytes 2097152 | tf_op jit(solution)/shard_map/psum | solution.py:9
  15.4 302.3 %copy-start.3 = (s32[1024]{0:T(1024)S(1)}, s32[1024]{0:T(1024)}, u32[]{:S(2)}) copy-start(s32[1024]{0:T(1024)} %param.5) | copy-start | bytes 12292
  664.8 1.6 copy-start.1
  665.0 1.4 copy-start.2
Sparse Core Ops, SparseCore 0:
  13.9 298.8 all-reduce.3
  317.9 345.8 all-reduce.5
Sparse Core Ops, SparseCore 1:
  17.3 134.3 all-gather.1
where the time goes:
time: 678 us
  waiting for transfers between devices  643 us (95%)
  between operations  15 us (2%)
  matrix products  8.25 us (1%)
    psum x1, waiting for transfers between devices, spread(): return lax.psum(block, axis)  345 us
    psum x1, waiting for transfers between devices, per_device(): pivot_block = lax.psum(picked, 'prow')  297 us
  transfers between devices with their start and end apart: 3, of which 2 were waited for; matrix products, arithmetic and copies ran while one was open for 0% of the time, Pallas kernels for 0%

commit v1 on v0

v1 whole, which is shorter than its diff:
```python
import jax
import jax.numpy as jnp
from jax import lax
from jax.experimental import pallas as pl
from jax.experimental.pallas import tpu as pltpu
from jax.sharding import PartitionSpec as P

MESH = pl.DeviceIdType.MESH
F32, BF16, I32 = jnp.float32, jnp.bfloat16, jnp.int32

ZH, Y, X, ZL, C = 4, 4, 4, 8, 2
ROWS, NB, COLS = 512, 1024, 128
BLK = ROWS // (X * ZL * C)
KC = 48
HK = KC // 2
SLOTS = ZH * Y * KC
CH, NCH = 64, 4
TILE = ROWS // X
NATURAL = (0, 3, 1, 2)
BITS = ZL.bit_length() - 1


def rev(s):
    return sum(((s >> j) & 1) << (BITS - 1 - j) for j in range(BITS))


def dot(a, b):
    return jnp.dot(a, b, preferred_element_type=F32)


def split(a):
    hi = a.astype(BF16)
    return hi, (a - hi.astype(F32)).astype(BF16)


def split3(a):
    hi = a.astype(BF16)
    rest = a - hi.astype(F32)
    mid = rest.astype(BF16)
    return hi, mid, (rest - mid.astype(F32)).astype(BF16)


def kernel(
    mat, pan_in, piv, out,
    pan, phi, plo, vloc, vfwd, vall, vhl, tt, thm, tlo, slots, slotc, phl,
    dall, dme, dfwd, base, ub, uhl, send, recv,
):
    prow, pcol = lax.axis_index("prow"), lax.axis_index("pcol")
    zh, y = prow // Y, prow % Y
    x, zl, c = pcol // (ZL * C), (pcol // C) % ZL, pcol % C

    def at(zh=zh, y=y, x=x, zl=zl, c=c):
        return (zh * Y + y, x * (ZL * C) + zl * C + c)

    def bit(j):
        return (zl // (1 << j)) % 2

    ydev = [at(y=(y + d) % Y) for d in range(Y)]
    xdev = [at(x=(x + d) % X) for d in range(X)]
    zdev = [at(zl=zl + (1 << j) - (2 << j) * bit(j)) for j in range(BITS)]
    other = at(c=1 - c)
    up, down = at(zh=(zh + 1) % ZH), at(zh=(zh + ZH - 1) % ZH)
    partners = ydev[1:] + xdev[1:] + zdev + [other, up, down]

    names = {}

    def num(key):
        return names.setdefault(key, len(names))

    counter = [0]

    def rc(src, dst, key, dev):
        sid = counter[0]
        counter[0] += 1
        return pltpu.make_async_remote_copy(
            src_ref=src, dst_ref=dst, send_sem=send.at[sid], recv_sem=recv.at[num(key)],
            device_id=dev, device_id_type=MESH,
        )

    def arrived(dst, key):
        pltpu.make_async_remote_copy(
            src_ref=dst, dst_ref=dst, send_sem=send.at[0], recv_sem=recv.at[num(key)],
            device_id=other, device_id_type=MESH,
        ).wait_recv()

    pending = []

    def start(copies, cond=None):
        pending.append((cond, copies))
        if cond is None:
            for cp in copies:
                cp.start()
        else:
            @pl.when(cond)
            def _():
                for cp in copies:
                    cp.start()

    barrier = pltpu.get_barrier_semaphore()
    for dev in partners:
        pl.semaphore_signal(barrier, inc=1, device_id=dev, device_id_type=MESH)

    prowv = piv[...]
    named = prowv >= NB
    group = (prowv // ROWS) % Y * ZH + (prowv // ROWS) // Y
    onehot = jnp.where(
        (lax.broadcasted_iota(I32, (ZH * Y, NB), 0) == group) & named, 1.0, 0.0
    ).astype(F32)
    tri = jnp.where(
        lax.broadcasted_iota(I32, (128, 128), 0) < lax.broadcasted_iota(I32, (128, 128), 1), 1.0, 0.0
    ).astype(BF16)
    before = jnp.zeros((ZH * Y, 1), F32)
    ranks = []
    for b in range(NB // 128):
        part = onehot[:, b * 128:(b + 1) * 128]
        count = dot(part.astype(BF16), tri) + before
        ranks.append(jnp.sum(count * part, axis=0, keepdims=True))
        before = before + jnp.sum(part, axis=1, keepdims=True)
    rank = jnp.concatenate(ranks, axis=1)
    slot = jnp.where(named, group.astype(F32) * KC + rank, -1.0)
    slots[...] = jnp.broadcast_to(slot, (8, NB))

    me = (y * ZH + zh) * KC
    kk = lax.broadcasted_iota(I32, (128, NB), 0)
    mine = (kk < KC) & ((kk + me).astype(F32) == slot)
    where_row = jnp.sum(
        jnp.where(mine, (prowv - prow * ROWS + 1).astype(F32), 0.0), axis=1, keepdims=True
    ) - 1.0
    pick = jnp.where(
        lax.broadcasted_iota(I32, (128, ROWS), 1).astype(F32) == where_row, 1.0, 0.0
    ).astype(F32)
    mh, mm, ml = split3(mat[...])
    pick16 = pick[:KC].astype(BF16)
    vloc[...] = (dot(pick16, mh) + dot(pick16, mm)) + dot(pick16, ml)
    dme[KC:, :] = jnp.zeros((128 - KC, COLS), F32)

    top = zh == 0
    root = top & (y < 2)
    inner = (zh == 1) | (zh == 3)

    @pl.when(top)
    def _():
        vall[y, 0] = vloc[...]

    @pl.when(root)
    def _():
        tt[y] = mat[...]

    pl.semaphore_wait(barrier, len(partners))

    s_own = sum(bit(j) * (1 << (BITS - 1 - j)) for j in range(BITS))
    j0 = BITS - 1
    pan[x, c, s_own] = pan_in[...]
    start([rc(pan_in, pan.at[x, c, s_own], "pz0", zdev[j0])])
    start([rc(vloc, vall.at[y, 1], "v1", down)], zh == 1)
    start([rc(vloc, vall.at[y, 3], "v3", up)], zh == 3)
    start([rc(vloc.at[pl.ds(0, HK)], vfwd, "vf", down),
           rc(vloc.at[pl.ds(HK, HK)], vfwd, "vf", up)], zh == 2)
    start([rc(mat, tt.at[0], "t0", ydev[1])], top & (y == 0))

    def to_roots(z):
        for d in range(1, Y):
            target = (y + d) % Y
            start([rc(vall.at[y, z], vall.at[y, z], ("vy", d, z), ydev[d])], top & (target < 2))

    to_roots(0)

    for t in range(BITS):
        j = BITS - 1 - t
        size = 1 << t
        base_in = (s_own // size) * size
        theirs = base_in + (size - 2 * size * ((s_own // size) % 2))
        arrived(pan.at[x, c, pl.ds(theirs, size)] if t else pan.at[x, c, theirs], ("pz%d" % t))
        if t + 1 < BITS:
            nxt = 2 * size
            have = (s_own // nxt) * nxt
            start([rc(pan.at[x, c, pl.ds(have, nxt)], pan.at[x, c, pl.ds(have, nxt)],
                      "pz%d" % (t + 1), zdev[j - 1])])
        if t == 1:
            @pl.when(inner)
            def _():
                arrived(vfwd, "vf")
            start([rc(vfwd, vall.at[y, 2, pl.ds(0, HK)], "v2a", down)], zh == 1)
            start([rc(vfwd, vall.at[y, 2, pl.ds(HK, HK)], "v2b", up)], zh == 3)

    for d in (2, 1, 3):
        start([rc(pan.at[x, c], pan.at[x, c], ("px", d), xdev[d])])
    start([rc(pan.at[x, c], pan.at[x, c], ("pc", 0), other)])

    @pl.when(top)
    def _():
        arrived(vall.at[y, 1], "v1")
    to_roots(1)

    @pl.when(top)
    def _():
        arrived(vall.at[y, 3], "v3")
    to_roots(3)

    @pl.when(root & (y == 1))
    def _():
        arrived(tt.at[0], "t0")

    @pl.when(root)
    def _():
        def tops(i, carry):
            for h in range(2):
                hi, mid, lo = split3(tt[h, pl.ds(i * 128, 128), :])
                at_row = pl.ds(h * ROWS + i * 128, 128)
                thm[at_row, 0:128] = hi
                thm[at_row, 128:256] = mid
                tlo[at_row, :] = lo
            return carry

        @pl.when(y == 0)
        def _():
            tt[1] = jnp.zeros((ROWS, COLS), F32)
        lax.fori_loop(0, ROWS // 128, tops, 0)

    @pl.when(root & (y == 1))
    def _():
        def pack(i, carry):
            ss = lax.broadcasted_iota(I32, (ZH * KC, NB), 0) + i * (ZH * KC)
            got = jnp.where(ss.astype(F32) == slots[0:1, :], 1.0, 0.0).astype(BF16)
            two = dot(got, thm[...])
            all3 = (two[:, :128] + two[:, 128:]) + dot(got, tlo[...])
            for z in range(ZH):
                dall[i, z] = all3[z * KC:(z + 1) * KC]
            return carry
        lax.fori_loop(0, Y, pack, 0)

    for d in range(1, Y):
        start([rc(dall.at[(y + d) % Y], dall.at[(y + d) % Y], "dy", ydev[d])], top & (y == 1))

    @pl.when(top)
    def _():
        arrived(vall.at[y, 2, pl.ds(0, HK)], "v2a")
        arrived(vall.at[y, 2, pl.ds(HK, HK)], "v2b")
    to_roots(2)

    @pl.when(top & (y != 1))
    def _():
        arrived(dall.at[y], "dy")
    start([rc(dall.at[y, 1], dme.at[pl.ds(0, KC)], "d", up),
           rc(dall.at[y, 3], dme.at[pl.ds(0, KC)], "d", down),
           rc(dall.at[y, 2, pl.ds(0, HK)], dfwd, "df", up),
           rc(dall.at[y, 2, pl.ds(HK, HK)], dfwd, "df", down)], top)

    @pl.when(root)
    def _():
        slotc[...] = jnp.transpose(jnp.broadcast_to(slots[0:1, :], (128, NB)))
        for d in range(1, Y):
            src = (y + Y - d) % Y
            for z in range(ZH):
                arrived(vall.at[src, z], ("vy", d, z))

        def vsplit(i, carry):
            for z in range(ZH):
                hi, lo = split(vall[i, z])
                vhl[pl.ds(i * (ZH * KC) + z * KC, KC), 0:128] = hi
                vhl[pl.ds(i * (ZH * KC) + z * KC, KC), 128:256] = lo
            return carry
        lax.fori_loop(0, Y, vsplit, 0)

        def form(i, carry):
            rows = pl.ds(i * 128, 128)
            sc = slotc[rows, :]
            lane = lax.broadcasted_iota(I32, (128, 128), 1)
            sel = jnp.concatenate(
                [jnp.where((lane + b * 128).astype(F32) == sc, 1.0, 0.0).astype(BF16)
                 for b in range(SLOTS // 128)], axis=1)
            moved = dot(sel, vhl[...])
            stay = jnp.concatenate([sc, sc], axis=1) < 0.0
            phl[rows, :] = jnp.where(stay, thm[rows, :].astype(F32), moved).astype(BF16)
            return carry

        @pl.when(y == 0)
        def _():
            phl[ROWS:, :] = jnp.zeros((ROWS, 2 * COLS), BF16)
        lax.fori_loop(0, 4 + 4 * y, form, 0)

    for d in (1, 3, 2):
        src = (x + X - d) % X
        arrived(pan.at[src, c], ("px", d))
        start([rc(pan.at[src, c], pan.at[src, c], ("pc", d), other)])
    for d in (0, 1, 3, 2):
        arrived(pan.at[(x + X - d) % X, 1 - c], ("pc", d))

    def psplit(i, carry):
        for cc in range(C):
            for s in range(ZL):
                hi, lo = split(pan[i, cc, s])
                rows = pl.ds((cc * ZL + s) * BLK, BLK)
                phi[i, rows, :] = hi
                plo[i, rows, :] = lo
        return carry
    lax.fori_loop(0, X, psplit, 0)

    def blocks(i, right, store):
        two = dot(phi[i], right[...])
        res = (two[:, :128] + two[:, 128:]) + dot(plo[i], right[:, 0:128])
        for cc in range(C):
            for s in range(ZL):
                k = cc * ZL + s
                store(i * TILE + BLK * (rev(s) * C + cc), res[k * BLK:(k + 1) * BLK])

    def u_half(h):
        line = y + h * (3 - 2 * y)

        @pl.when(root)
        def _():
            def store(row, val):
                ub[line, pl.ds(row - h * (ROWS // 2), BLK), :] = val
                out[pl.ds(row, BLK), :] = val

            def tile(i, carry):
                blocks(i, phl, store)
                return carry
            lax.fori_loop(2 * h, 2 * h + 2, tile, 0)

    def chunk(line, k):
        return ub.at[line, pl.ds(k * CH, CH)]

    def send_u(line, k, dev, cond):
        start([rc(chunk(line, k), chunk(line, k), ("u", k, "line"), dev)], cond)

    def ukey(rel, k):
        return ("u", rel, k)

    def send_chunk(line, rel, k, dev, cond):
        start([rc(chunk(line, k), chunk(line, k), ukey(rel, k), dev)], cond)

    r0, r1 = top & (y == 0), top & (y == 1)
    u_half(1)
    for k in range(NCH):
        send_chunk(3, 0, k, ydev[3], r0)
        send_chunk(2, 0, k, ydev[1], r1)
    u_half(0)
    order_up, order_down = (0, 1, 2, 3), (2, 3, 0, 1)
    for a, b in zip(order_up, order_down):
        send_chunk(y, 0, a, up, root)
        send_chunk(y, 0, b, down, root)
    for k in range(NCH):
        send_chunk(3, 1, k, ydev[2], r0)
        send_chunk(0, 2, k, ydev[2], r0)
        send_chunk(0, 1, k, ydev[3], r0)
        send_chunk(1, 3, k, ydev[1], r1)
        send_chunk(1, 2, k, ydev[2], r1)
        send_chunk(2, 3, k, ydev[2], r1)

    nonroot = top & (y >= 2)
    for a, b in zip(order_up, order_down):
        @pl.when(nonroot)
        def _():
            if a < 2:
                arrived(chunk(y, a), ukey(0, a))
                arrived(chunk(y, b), ukey(0, b))
        send_chunk(y, 0, a, up, nonroot)
        send_chunk(y, 0, b, down, nonroot)

    @pl.when(inner)
    def _():
        arrived(dfwd, "df")
    start([rc(dfwd, dme.at[pl.ds(0, HK)], "d2a", up)], zh == 1)
    start([rc(dfwd, dme.at[pl.ds(HK, HK)], "d2b", down)], zh == 3)

    @pl.when(nonroot)
    def _():
        dme[0:KC, :] = dall[y, 0]

    @pl.when(inner)
    def _():
        arrived(dme.at[pl.ds(0, KC)], "d")

    @pl.when(zh == 2)
    def _():
        arrived(dme.at[pl.ds(0, HK)], "d2a")
        arrived(dme.at[pl.ds(HK, HK)], "d2b")

    notroot = (zh > 0) | (y >= 2)

    @pl.when(notroot)
    def _():
        scat = jnp.transpose(pick)
        hit = jnp.sum(scat, axis=1, keepdims=True) > 0.0
        dh, dm, dl = split3(dme[...])
        scat16 = scat.astype(BF16)
        moved = (dot(scat16, dh) + dot(scat16, dm)) + dot(scat16, dl)
        base[...] = jnp.where(hit, moved, mat[...])

    for z, order in ((1, order_up), (3, order_down), (2, (0, 2, 1, 3))):
        for k in order:
            @pl.when(zh == z)
            def _():
                arrived(chunk(y, k), ukey(0, k))
            if z == 1 and k < 2:
                send_chunk(y, 0, k, up, zh == 1)
            if z == 3 and k >= 2:
                send_chunk(y, 0, k, down, zh == 3)
            for d in (2, 1, 3):
                send_chunk(y, Y - d, k, ydev[d], zh == z)

    @pl.when(notroot)
    def _():
        for rel in range(1, Y):
            for k in range(NCH):
                arrived(chunk((y + rel) % Y, k), ukey(rel, k))

        for q, line in enumerate(NATURAL):
            hi, lo = split(ub[line])
            uhl[q * 256:(q + 1) * 256, 0:128] = hi
            uhl[q * 256:(q + 1) * 256, 128:256] = lo

        def store(row, val):
            out[pl.ds(row, BLK), :] = base[pl.ds(row, BLK), :] - val

        def tile(i, carry):
            blocks(i, uhl, store)
            return carry
        lax.fori_loop(0, X, tile, 0)

    for cond, copies in pending:
        if cond is None:
            for cp in copies:
                cp.wait_send()
        else:
            @pl.when(cond)
            def _(copies=copies):
                for cp in copies:
                    cp.wait_send()


def per_device(matrix, panel, pivots):
    vmem = pl.BlockSpec(memory_space=pltpu.VMEM)
    return pl.pallas_call(
        kernel,
        out_shape=jax.ShapeDtypeStruct((ROWS, COLS), F32),
        in_specs=[vmem] * 3,
        out_specs=vmem,
        scratch_shapes=[
            pltpu.VMEM((X, C, ZL, BLK, NB), F32),
            pltpu.VMEM((X, TILE, NB), BF16),
            pltpu.VMEM((X, TILE, NB), BF16),
            pltpu.VMEM((KC, COLS), F32),
            pltpu.VMEM((HK, COLS), F32),
            pltpu.VMEM((Y, ZH, KC, COLS), F32),
            pltpu.VMEM((SLOTS, 2 * COLS), BF16),
            pltpu.VMEM((2, ROWS, COLS), F32),
            pltpu.VMEM((NB, 2 * COLS), BF16),
            pltpu.VMEM((NB, COLS), BF16),
            pltpu.VMEM((8, NB), F32),
            pltpu.VMEM((NB, 128), F32),
            pltpu.VMEM((NB, 2 * COLS), BF16),
            pltpu.VMEM((Y, ZH, KC, COLS), F32),
            pltpu.VMEM((128, COLS), F32),
            pltpu.VMEM((HK, COLS), F32),
            pltpu.VMEM((ROWS, COLS), F32),
            pltpu.VMEM((4, ROWS // 2, COLS), F32),
            pltpu.VMEM((NB, 2 * COLS), BF16),
            pltpu.SemaphoreType.DMA((192,)),
            pltpu.SemaphoreType.DMA((64,)),
        ],
        compiler_params=pltpu.CompilerParams(
            collective_id=0, has_side_effects=True, vmem_limit_bytes=40 * 2**20
        ),
    )(matrix, panel, pivots.reshape(1, NB))


def solution(mesh):
    placed = (P("prow", "pcol"), P(("prow", "pcol"), None), P())
    return jax.shard_map(
        per_device, mesh=mesh, in_specs=placed, out_specs=P("prow", "pcol"), check_vma=False
    )
```

time: 678 us -> 97.9 us (0.14)
  the two profiles are of different devices: /device:TPU:216 before, /device:TPU:704 now
where the time goes in v1:
time: 97.9 us; the launch traced here: 97.6 us
  Pallas kernels  94.5 us (97%)
  local copies, waits for them, and re-layouts  3.1 us (3%)
    pallas_call x1, Pallas kernels, per_device(): pl.pallas_call(kernel, out_shape=jax.ShapeDtypeStruct((ROWS, COLS), F32),...  94.5 us
    unnamed x7, local copies, waits for them, and re-layouts  3.1 us

profile of v1, /device:TPU:704, one launch (start us, length us, event | category | flops | bytes accessed | tf_op | source)
XLA Modules:
  0.0 97.6 jit_solution(11857852809616760258)
XLA Ops:
  0.0 0.0 copy-start
  0.0 0.9 copy-done
  1.0 0.0 copy-start.1
  1.0 0.8 copy-done.1
  1.7 0.0 copy-start.2
  1.7 0.7 copy-done.2
  2.4 94.5 %shard_map.37 = f32[512,128]{1,0:T(8,128)S(1)} custom-call(f32[512,128]{1,0:T(8,128)S(1)} %copy-done, f32[8,1024]{1,0:T(8,128)S(1)} %copy-done.1, s32[1,1024]{1,0:T(1,128)S(1)} %bitcast.1), custom_call_target="tpu_custom_call" | custom-call | tf_op jit(solution)/shard_map/pallas_call | solution.py:435
  96.9 0.7 copy.5
Async XLA Ops:
  0.0 0.9 copy-start
  1.0 0.8 copy-start.1
  1.7 0.7 copy-start.2

commit v2 on v1

v2 whole, which is shorter than its diff:
```python
import jax
import jax.numpy as jnp
from jax import lax
from jax.experimental import pallas as pl
from jax.experimental.pallas import tpu as pltpu
from jax.sharding import PartitionSpec as P

MESH = pl.DeviceIdType.MESH
F32, BF16, I32 = jnp.float32, jnp.bfloat16, jnp.int32

ZH, Y, X, ZL, C = 4, 4, 4, 8, 2
ROWS, NB, COLS = 512, 1024, 128
BLK = ROWS // (X * ZL * C)
KC = 48
SLOTS = ZH * Y * KC
CH, NCH = 64, 4
TILE = ROWS // X
NATURAL = (0, 3, 1, 2)
BITS = ZL.bit_length() - 1
HALF = ZL // 2
QR = NB // 4


def rev(s):
    return sum(((s >> j) & 1) << (BITS - 1 - j) for j in range(BITS))


def dot(a, b):
    return jnp.dot(a, b, preferred_element_type=F32)


def split(a):
    hi = a.astype(BF16)
    return hi, (a - hi.astype(F32)).astype(BF16)


def split3(a):
    hi = a.astype(BF16)
    rest = a - hi.astype(F32)
    mid = rest.astype(BF16)
    return hi, mid, (rest - mid.astype(F32)).astype(BF16)


def kernel(
    mat_hbm, pan_hbm, piv_hbm, out,
    mat, piv, pan, phi, plo, vloc, vall, vhl, tt, thm, tlo, slots, slotc, phl,
    dall, dme, dfwd, scat, base, ub, uhl, send, recv, local,
):
    prow, pcol = lax.axis_index("prow"), lax.axis_index("pcol")
    zh, y = prow // Y, prow % Y
    x, zl, c = pcol // (ZL * C), (pcol // C) % ZL, pcol % C

    def at(zh=zh, y=y, x=x, zl=zl, c=c):
        return (zh * Y + y, x * (ZL * C) + zl * C + c)

    def bit(j):
        return (zl // (1 << j)) % 2

    ydev = [at(y=(y + d) % Y) for d in range(Y)]
    xdev = [at(x=(x + d) % X) for d in range(X)]
    zdev = [at(zl=zl + (1 << j) - (2 << j) * bit(j)) for j in range(BITS)]
    other = at(c=1 - c)
    up, down = at(zh=(zh + 1) % ZH), at(zh=(zh + ZH - 1) % ZH)
    near = ydev[1:] + xdev[1:] + zdev + [other]

    names = {}

    def num(key):
        return names.setdefault(key, len(names))

    counter = [0]

    def rc(src, dst, key, dev):
        sid = counter[0]
        counter[0] += 1
        return pltpu.make_async_remote_copy(
            src_ref=src, dst_ref=dst, send_sem=send.at[sid], recv_sem=recv.at[num(key)],
            device_id=dev, device_id_type=MESH,
        )

    def arrived(dst, key):
        pltpu.make_async_remote_copy(
            src_ref=dst, dst_ref=dst, send_sem=send.at[0], recv_sem=recv.at[num(key)],
            device_id=other, device_id_type=MESH,
        ).wait_recv()

    pending = []

    def start(copies, cond=None):
        pending.append((cond, copies))
        if cond is None:
            for cp in copies:
                cp.start()
        else:
            @pl.when(cond)
            def _():
                for cp in copies:
                    cp.start()

    top = zh == 0
    root = top & (y < 2)
    notroot = (zh > 0) | (y >= 2)
    inner = (zh == 1) | (zh == 3)
    early = zl < ZL // 2

    barrier = pltpu.get_barrier_semaphore()

    @pl.when(top)
    def _():
        for z in (2, 1, 3):
            pl.semaphore_signal(barrier, inc=1, device_id=at(zh=z), device_id_type=MESH)
    for dev in near:
        pl.semaphore_signal(barrier, inc=1, device_id=dev, device_id_type=MESH)

    s_own = sum(bit(j) * (1 << (BITS - 1 - j)) for j in range(BITS))
    own = pan.at[x, c, s_own]
    loads = [pltpu.make_async_copy(piv_hbm, piv, local.at[0]),
             pltpu.make_async_copy(mat_hbm, mat, local.at[1]),
             pltpu.make_async_copy(pan_hbm, own, local.at[2])]
    for cp in loads:
        cp.start()
    loads[0].wait()

    def pack_own(prowv, slot):
        me = (y * ZH + zh) * KC
        kk = lax.broadcasted_iota(I32, (128, NB), 0)
        mine = (kk < KC) & ((kk + me).astype(F32) == slot)
        where_row = jnp.sum(
            jnp.where(mine, (prowv - prow * ROWS + 1).astype(F32), 0.0), axis=1, keepdims=True
        ) - 1.0
        pick = jnp.where(
            lax.broadcasted_iota(I32, (128, ROWS), 1).astype(F32) == where_row, 1.0, 0.0
        ).astype(F32)
        mh, mm, ml = split3(mat[...])
        pick16 = pick[:KC].astype(BF16)
        vloc[...] = (dot(pick16, mh) + dot(pick16, mm)) + dot(pick16, ml)
        scat[...] = jnp.transpose(pick).astype(BF16)

    prowv = piv[...]
    named = prowv >= NB
    group = (prowv // ROWS) % Y * ZH + (prowv // ROWS) // Y
    onehot = jnp.where(
        (lax.broadcasted_iota(I32, (ZH * Y, NB), 0) == group) & named, 1.0, 0.0
    ).astype(F32)
    tri = jnp.where(
        lax.broadcasted_iota(I32, (128, 128), 0) < lax.broadcasted_iota(I32, (128, 128), 1), 1.0, 0.0
    ).astype(BF16)
    before = jnp.zeros((ZH * Y, 1), F32)
    ranks = []
    for b in range(NB // 128):
        part = onehot[:, b * 128:(b + 1) * 128]
        count = dot(part.astype(BF16), tri) + before
        ranks.append(jnp.sum(count * part, axis=0, keepdims=True))
        before = before + jnp.sum(part, axis=1, keepdims=True)
    rank = jnp.concatenate(ranks, axis=1)
    slot = jnp.where(named, group.astype(F32) * KC + rank, -1.0)
    slots[...] = jnp.broadcast_to(slot, (8, NB))

    loads[1].wait()

    @pl.when(root)
    def _():
        vloc[...] = jnp.zeros((KC, COLS), F32)
        tt[y] = mat[...]

    @pl.when(notroot)
    def _():
        pack_own(prowv, slot)
    dme[KC:, :] = jnp.zeros((128 - KC, COLS), F32)

    @pl.when(top)
    def _():
        vall[y, 0] = vloc[...]

    loads[2].wait()
    pl.semaphore_wait(barrier, len(near) + (zh + ZH - 1) // ZH)

    j0 = BITS - 1
    start([rc(own, own, "pz0", zdev[j0])])
    start([rc(vloc, vall.at[y, 1], "v1", down)], zh == 1)
    start([rc(vloc, vall.at[y, 3], "v3", up)], zh == 3)
    start([rc(vloc, vall.at[y, 2], "v2", at(zh=(zh + 2) % ZH))], zh == 2)
    start([rc(mat, tt.at[0], "t0", ydev[1])], top & (y == 0))

    def to_roots(z):
        for d in range(1, Y):
            target = (y + d) % Y
            start([rc(vall.at[y, z], vall.at[y, z], ("vy", d, z), ydev[d])], top & (target < 2))

    to_roots(0)

    def to_core(d, piece, first):
        blocks = pan.at[(x + X - d) % X, c, pl.ds(first, HALF)]
        start([rc(blocks, blocks, ("pc", d, piece), other)])

    def over_x(piece, first):
        blocks = pan.at[x, c, pl.ds(first, HALF)]
        for d in (2, 1, 3):
            start([rc(blocks, blocks, ("px", d, piece), xdev[d])])
        to_core(0, piece, first)

    for t in range(BITS):
        j = BITS - 1 - t
        size = 1 << t
        base_in = (s_own // size) * size
        theirs = base_in + (size - 2 * size * ((s_own // size) % 2))
        arrived(pan.at[x, c, pl.ds(theirs, size)] if t else pan.at[x, c, theirs], ("pz%d" % t))
        if t + 1 < BITS:
            nxt = 2 * size
            have = (s_own // nxt) * nxt
            start([rc(pan.at[x, c, pl.ds(have, nxt)], pan.at[x, c, pl.ds(have, nxt)],
                      "pz%d" % (t + 1), zdev[j - 1])])
        if t + 2 == BITS:
            over_x(0, have)

    over_x(1, theirs)

    @pl.when(root & (y == 1))
    def _():
        arrived(tt.at[0], "t0")

    @pl.when(root)
    def _():
        def tops(i, carry):
            for h in range(2):
                hi, mid, lo = split3(tt[h, pl.ds(i * 128, 128), :])
                at_row = pl.ds(h * ROWS + i * 128, 128)
                thm[at_row, 0:128] = hi
                thm[at_row, 128:256] = mid
                tlo[at_row, :] = lo
            return carry

        @pl.when(y == 0)
        def _():
            tt[1] = jnp.zeros((ROWS, COLS), F32)
        lax.fori_loop(0, ROWS // 128, tops, 0)

    @pl.when(root & (y == 1))
    def _():
        def pack(i, carry):
            ss = lax.broadcasted_iota(I32, (ZH * KC, NB), 0) + i * (ZH * KC)
            got = jnp.where(ss.astype(F32) == slots[0:1, :], 1.0, 0.0).astype(BF16)
            two = dot(got, thm[...])
            all3 = (two[:, :128] + two[:, 128:]) + dot(got, tlo[...])
            for z in range(ZH):
                dall[i, z] = all3[z * KC:(z + 1) * KC]
            return carry
        lax.fori_loop(0, Y, pack, 0)

    for d in range(1, Y):
        start([rc(dall.at[(y + d) % Y], dall.at[(y + d) % Y], "dy", ydev[d])], top & (y == 1))

    for z in (1, 3):
        @pl.when(top)
        def _():
            arrived(vall.at[y, z], "v%d" % z)
        to_roots(z)

    for d in (1, 3, 2):
        src = (x + X - d) % X
        arrived(pan.at[src, c, pl.ds(have, HALF)], ("px", d, 0))
        to_core(d, 0, have)

    @pl.when(top & (y != 1))
    def _():
        arrived(dall.at[y], "dy")
    start([rc(dall.at[y, 1], dme.at[pl.ds(0, KC)], "d", up),
           rc(dall.at[y, 3], dme.at[pl.ds(0, KC)], "d", down)], top)

    for d in (1, 3, 2):
        src = (x + X - d) % X
        arrived(pan.at[src, c, pl.ds(theirs, HALF)], ("px", d, 1))
        to_core(d, 1, theirs)

    @pl.when(top)
    def _():
        arrived(vall.at[y, 2], "v2")
    to_roots(2)
    start([rc(dall.at[y, 2], dfwd, "df", up)], top & early)
    start([rc(dall.at[y, 2], dfwd, "df", down)], top & (zl >= ZL // 2))

    for piece, mine_at in enumerate((have, theirs)):
        for d in range(X):
            arrived(pan.at[(x + X - d) % X, 1 - c, pl.ds(mine_at, HALF)], ("pc", d, piece))

    def psplit(i, carry):
        for cc in range(C):
            for s in range(ZL):
                hi, lo = split(pan[i, cc, s])
                rows = pl.ds((cc * ZL + s) * BLK, BLK)
                for q, line in enumerate(NATURAL):
                    phi[i, rows, line * QR:(line + 1) * QR] = hi[:, q * QR:(q + 1) * QR]
                    plo[i, rows, line * QR:(line + 1) * QR] = lo[:, q * QR:(q + 1) * QR]
        return carry
    lax.fori_loop(0, X, psplit, 0)

    @pl.when(root)
    def _():
        slotc[...] = jnp.transpose(jnp.broadcast_to(slots[0:1, :], (128, NB)))
        for d in range(1, Y):
            src = (y + Y - d) % Y
            for z in range(ZH):
                arrived(vall.at[src, z], ("vy", d, z))

        def vsplit(i, carry):
            for z in range(ZH):
                hi, lo = split(vall[i, z])
                vhl[pl.ds(i * (ZH * KC) + z * KC, KC), 0:128] = hi
                vhl[pl.ds(i * (ZH * KC) + z * KC, KC), 128:256] = lo
            return carry
        lax.fori_loop(0, Y, vsplit, 0)

        def form(i, q, line):
            rows = pl.ds(q * QR + i * 128, 128)
            sc = slotc[rows, :]
            lane = lax.broadcasted_iota(I32, (128, 128), 1)
            sel = jnp.concatenate(
                [jnp.where((lane + b * 128).astype(F32) == sc, 1.0, 0.0).astype(BF16)
                 for b in range(SLOTS // 128)], axis=1)
            moved = dot(sel, vhl[...])
            stay = jnp.concatenate([sc, sc], axis=1) < 0.0
            phl[pl.ds(line * QR + i * 128, 128), :] = jnp.where(
                stay, thm[rows, :].astype(F32), moved).astype(BF16)

        def form_two(q, line):
            def body(i, carry):
                form(i, q, line)
                return carry
            lax.fori_loop(0, 2, body, 0)

        form_two(0, NATURAL[0])
        form_two(1, NATURAL[1])

        @pl.when(y == 0)
        def _():
            for line in NATURAL[2:]:
                phl[line * QR:(line + 1) * QR, :] = jnp.zeros((QR, 2 * COLS), BF16)

        @pl.when(y == 1)
        def _():
            form_two(2, NATURAL[2])
            form_two(3, NATURAL[3])

    def blocks(i, right, store, cols=slice(None)):
        two = dot(phi[i, :, cols], right[...])
        res = (two[:, :128] + two[:, 128:]) + dot(plo[i, :, cols], right[:, 0:128])
        for cc in range(C):
            for s in range(ZL):
                k = cc * ZL + s
                store(i * TILE + BLK * (rev(s) * C + cc), res[k * BLK:(k + 1) * BLK])

    def u_tile(i):
        h = i // 2
        line = y + h * (3 - 2 * y)

        @pl.when(root)
        def _():
            def store(row, val):
                ub[line, pl.ds(row - h * QR, BLK), :] = val
                out[pl.ds(row, BLK), :] = val
            blocks(i, phl, store)

    def chunk(line, k):
        return ub.at[line, pl.ds(k * CH, CH)]

    def ukey(rel, k):
        return ("u", rel, k)

    def send_chunk(line, rel, k, dev, cond):
        start([rc(chunk(line, k), chunk(line, k), ukey(rel, k), dev)], cond)

    r0, r1 = top & (y == 0), top & (y == 1)
    per = TILE // CH
    for i in (2, 3, 0, 1):
        u_tile(i)
        for k in range((i % 2) * per, (i % 2 + 1) * per):
            if i >= 2:
                send_chunk(3, 0, k, ydev[3], r0)
                send_chunk(2, 0, k, ydev[1], r1)
            else:
                send_chunk(y, 0, k, up, root)
                send_chunk(y, 0, k, down, root)
    for k in range(NCH):
        send_chunk(3, 1, k, ydev[2], r0)
        send_chunk(0, 2, k, ydev[2], r0)
        send_chunk(0, 1, k, ydev[3], r0)
        send_chunk(1, 3, k, ydev[1], r1)
        send_chunk(1, 2, k, ydev[2], r1)
        send_chunk(2, 3, k, ydev[2], r1)

    nonroot = top & (y >= 2)
    for k in range(NCH):
        @pl.when(nonroot)
        def _():
            arrived(chunk(y, k), ukey(0, k))
        send_chunk(y, 0, k, up, nonroot)
        send_chunk(y, 0, k, down, nonroot)

    via1, via3 = (zh == 1) & early, (zh == 3) & (zl >= ZL // 2)

    @pl.when(via1 | via3)
    def _():
        arrived(dfwd, "df")
    start([rc(dfwd, dme.at[pl.ds(0, KC)], "d", up)], via1)
    start([rc(dfwd, dme.at[pl.ds(0, KC)], "d", down)], via3)

    @pl.when(nonroot)
    def _():
        dme[0:KC, :] = dall[y, 0]

    @pl.when(zh > 0)
    def _():
        arrived(dme.at[pl.ds(0, KC)], "d")

    @pl.when(notroot)
    def _():
        hit = jnp.sum(scat[...].astype(F32), axis=1, keepdims=True) > 0.0
        dh, dm, dl = split3(dme[...])
        moved = (dot(scat[...], dh) + dot(scat[...], dm)) + dot(scat[...], dl)
        base[...] = jnp.where(hit, moved, mat[...])

    for k in range(NCH):
        @pl.when(zh > 0)
        def _():
            arrived(chunk(y, k), ukey(0, k))
        send_chunk(y, 0, k, up, via1)
        send_chunk(y, 0, k, down, via3)
        for d in (2, 1, 3):
            send_chunk(y, Y - d, k, ydev[d], zh > 0)

    @pl.when(notroot)
    def _():
        def line_step(line, last):
            hi, lo = split(ub[line])
            uhl[:, 0:128] = hi
            uhl[:, 128:256] = lo
            at_col = pl.ds(pl.multiple_of(line * QR, QR), QR)

            def store(row, val):
                rows = pl.ds(row, BLK)
                if last:
                    out[rows, :] = base[rows, :] - val
                else:
                    base[rows, :] = base[rows, :] - val

            def tile(i, carry):
                blocks(i, uhl, store, at_col)
                return carry
            lax.fori_loop(0, X, tile, 0)

        line_step(y, False)
        for rel in (1, 3, 2):
            for k in range(NCH):
                arrived(chunk((y + rel) % Y, k), ukey(rel, k))
            line_step((y + rel) % Y, rel == 2)

    for cond, copies in pending:
        if cond is None:
            for cp in copies:
                cp.wait_send()
        else:
            @pl.when(cond)
            def _(copies=copies):
                for cp in copies:
                    cp.wait_send()


def per_device(matrix, panel, pivots):
    hbm, vmem = pl.BlockSpec(memory_space=pltpu.HBM), pl.BlockSpec(memory_space=pltpu.VMEM)
    return pl.pallas_call(
        kernel,
        out_shape=jax.ShapeDtypeStruct((ROWS, COLS), F32),
        in_specs=[hbm] * 3,
        out_specs=vmem,
        scratch_shapes=[
            pltpu.VMEM((ROWS, COLS), F32),
            pltpu.VMEM((1, NB), I32),
            pltpu.VMEM((X, C, ZL, BLK, NB), F32),
            pltpu.VMEM((X, TILE, NB), BF16),
            pltpu.VMEM((X, TILE, NB), BF16),
            pltpu.VMEM((KC, COLS), F32),
            pltpu.VMEM((Y, ZH, KC, COLS), F32),
            pltpu.VMEM((SLOTS, 2 * COLS), BF16),
            pltpu.VMEM((2, ROWS, COLS), F32),
            pltpu.VMEM((NB, 2 * COLS), BF16),
            pltpu.VMEM((NB, COLS), BF16),
            pltpu.VMEM((8, NB), F32),
            pltpu.VMEM((NB, 128), F32),
            pltpu.VMEM((NB, 2 * COLS), BF16),
            pltpu.VMEM((Y, ZH, KC, COLS), F32),
            pltpu.VMEM((128, COLS), F32),
            pltpu.VMEM((KC, COLS), F32),
            pltpu.VMEM((ROWS, 128), BF16),
            pltpu.VMEM((ROWS, COLS), F32),
            pltpu.VMEM((4, ROWS // 2, COLS), F32),
            pltpu.VMEM((QR, 2 * COLS), BF16),
            pltpu.SemaphoreType.DMA((192,)),
            pltpu.SemaphoreType.DMA((64,)),
            pltpu.SemaphoreType.DMA((3,)),
        ],
        compiler_params=pltpu.CompilerParams(
            collective_id=0, has_side_effects=True, vmem_limit_bytes=40 * 2**20
        ),
    )(matrix, panel, pivots.reshape(1, NB))


def solution(mesh):
    placed = (P("prow", "pcol"), P(("prow", "pcol"), None), P())
    return jax.shard_map(
        per_device, mesh=mesh, in_specs=placed, out_specs=P("prow", "pcol"), check_vma=False
    )
```

time: 97.9 us -> 75 us (0.77)
  the two profiles are of different devices: /device:TPU:704 before, /device:TPU:640 now
where the time goes in v2:
time: 75 us; the launch traced here: 74.7 us
  Pallas kernels  71.6 us (95%)
  local copies, waits for them, and re-layouts  3.1 us (4%)
    pallas_call x1, Pallas kernels, per_device(): pl.pallas_call(kernel, out_shape=jax.ShapeDtypeStruct((ROWS, COLS), F32),...  71.6 us
    unnamed x7, local copies, waits for them, and re-layouts  3.1 us

profile of v2, /device:TPU:640, one launch (start us, length us, event | category | flops | bytes accessed | tf_op | source)
XLA Modules:
  0.0 74.7 jit_solution(8120807570667057968)
XLA Ops:
  0.0 0.0 copy-start
  0.0 0.9 %copy-done = f32[512,128]{1,0:T(8,128)S(1)} copy-done((f32[512,128]{1,0:T(8,128)S(1)}, f32[512,128]{1,0:T(8,128)}, u32[]{:S(2)}) %copy-start) | copy-done | bytes 262168
  1.0 0.0 copy-start.1
  1.0 0.8 %copy-done.1 = f32[8,1024]{1,0:T(8,128)S(1)} copy-done((f32[8,1024]{1,0:T(8,128)S(1)}, f32[8,1024]{1,0:T(8,128)}, u32[]{:S(2)}) %copy-start.1) | copy-done | bytes 32792
  1.7 0.0 copy-start.2
  1.7 0.7 copy-done.2
  2.4 71.6 %shard_map.37 = f32[512,128]{1,0:T(8,128)S(1)} custom-call(f32[512,128]{1,0:T(8,128)S(1)} %copy-done, f32[8,1024]{1,0:T(8,128)S(1)} %copy-done.1, s32[1,1024]{1,0:T(1,128)S(1)} %bitcast.1), custom_call_target="tpu_custom_call" | custom-call | tf_op jit(solution)/shard_map/pallas_call | solution.py:470
  74.0 0.7 copy.5
Async XLA Ops:
  0.0 0.9 %copy-start = (f32[512,128]{1,0:T(8,128)S(1)}, f32[512,128]{1,0:T(8,128)}, u32[]{:S(2)}) copy-start(f32[512,128]{1,0:T(8,128)} %mat_hbm.1) | copy-start | bytes 786436
  1.0 0.8 %copy-start.1 = (f32[8,1024]{1,0:T(8,128)S(1)}, f32[8,1024]{1,0:T(8,128)}, u32[]{:S(2)}) copy-start(f32[8,1024]{1,0:T(8,128)} %pan_hbm.1) | copy-start | bytes 98308
  1.7 0.7 copy-start.2

commit v3 on v2

--- a/solution.py
+++ b/solution.py
@@ -19,6 +19,8 @@
 BITS = ZL.bit_length() - 1
 HALF = ZL // 2
 QR = NB // 4
+MIDDLE = 4
+UPS = 5
 
 
 def rev(s):
@@ -44,7 +46,7 @@
 def kernel(
     mat_hbm, pan_hbm, piv_hbm, out,
     mat, piv, pan, phi, plo, vloc, vall, vhl, tt, thm, tlo, slots, slotc, phl,
-    dall, dme, dfwd, scat, base, ub, uhl, send, recv, local,
+    dall, dme, dfwd, scat, sel, base, ub, uhl, send, recv, local, token,
 ):
     prow, pcol = lax.axis_index("prow"), lax.axis_index("pcol")
     zh, y = prow // Y, prow % Y
@@ -101,7 +103,10 @@
     root = top & (y < 2)
     notroot = (zh > 0) | (y >= 2)
     inner = (zh == 1) | (zh == 3)
-    early = zl < ZL // 2
+    high = zl // UPS
+    first = at(zh=3 - 2 * high)
+    second = at(zh=1 + 2 * high)
+    via1, via3 = (zh == 1) & (high == 1), (zh == 3) & (high == 0)
 
     barrier = pltpu.get_barrier_semaphore()
 
@@ -234,6 +239,16 @@
         def _():
             tt[1] = jnp.zeros((ROWS, COLS), F32)
         lax.fori_loop(0, ROWS // 128, tops, 0)
+        slotc[...] = jnp.transpose(jnp.broadcast_to(slots[0:1, :], (128, NB)))
+
+        def choose(i, carry):
+            rows = pl.ds(i * 128, 128)
+            lane = lax.broadcasted_iota(I32, (128, 128), 1)
+            for b in range(SLOTS // 128):
+                sel[rows, b * 128:(b + 1) * 128] = jnp.where(
+                    (lane + b * 128).astype(F32) == slotc[rows, :], 1.0, 0.0).astype(BF16)
+            return carry
+        lax.fori_loop(0, 4 + 4 * y, choose, 0)
 
     @pl.when(root & (y == 1))
     def _():
@@ -276,8 +291,7 @@
     def _():
         arrived(vall.at[y, 2], "v2")
     to_roots(2)
-    start([rc(dall.at[y, 2], dfwd, "df", up)], top & early)
-    start([rc(dall.at[y, 2], dfwd, "df", down)], top & (zl >= ZL // 2))
+    start([rc(dall.at[y, 2], dfwd, "df", first)], top)
 
     for piece, mine_at in enumerate((have, theirs)):
         for d in range(X):
@@ -296,7 +310,6 @@
 
     @pl.when(root)
     def _():
-        slotc[...] = jnp.transpose(jnp.broadcast_to(slots[0:1, :], (128, NB)))
         for d in range(1, Y):
             src = (y + Y - d) % Y
             for z in range(ZH):
@@ -313,11 +326,7 @@
         def form(i, q, line):
             rows = pl.ds(q * QR + i * 128, 128)
             sc = slotc[rows, :]
-            lane = lax.broadcasted_iota(I32, (128, 128), 1)
-            sel = jnp.concatenate(
-                [jnp.where((lane + b * 128).astype(F32) == sc, 1.0, 0.0).astype(BF16)
-                 for b in range(SLOTS // 128)], axis=1)
-            moved = dot(sel, vhl[...])
+            moved = dot(sel[rows, :], vhl[...])
             stay = jnp.concatenate([sc, sc], axis=1) < 0.0
             phl[pl.ds(line * QR + i * 128, 128), :] = jnp.where(
                 stay, thm[rows, :].astype(F32), moved).astype(BF16)
@@ -368,6 +377,13 @@
 
     def send_chunk(line, rel, k, dev, cond):
         start([rc(chunk(line, k), chunk(line, k), ukey(rel, k), dev)], cond)
+
+    firsts = [rc(chunk(y, k), chunk(y, k), ukey(0, k), first) for k in range(NCH)]
+
+    def send_first(k, cond):
+        @pl.when(cond)
+        def _():
+            firsts[k].start()
 
     r0, r1 = top & (y == 0), top & (y == 1)
     per = TILE // CH
@@ -378,8 +394,7 @@
                 send_chunk(3, 0, k, ydev[3], r0)
                 send_chunk(2, 0, k, ydev[1], r1)
             else:
-                send_chunk(y, 0, k, up, root)
-                send_chunk(y, 0, k, down, root)
+                send_first(k, root & (zl != MIDDLE))
     for k in range(NCH):
         send_chunk(3, 1, k, ydev[2], r0)
         send_chunk(0, 2, k, ydev[2], r0)
@@ -393,10 +408,39 @@
         @pl.when(nonroot)
         def _():
             arrived(chunk(y, k), ukey(0, k))
-        send_chunk(y, 0, k, up, nonroot)
-        send_chunk(y, 0, k, down, nonroot)
-
-    via1, via3 = (zh == 1) & early, (zh == 3) & (zl >= ZL // 2)
+        send_first(k, nonroot & (zl != MIDDLE))
+
+    @pl.when(top & (zl == MIDDLE))
+    def _():
+        pl.semaphore_wait(token.at[1], 1)
+        for cp in firsts:
+            cp.start()
+
+    @pl.when(top)
+    def _():
+        @pl.when(zl == ZL - 1)
+        def _():
+            for q in range(MIDDLE, -1, -1):
+                pl.semaphore_signal(token.at[0], inc=1, device_id=at(zl=q), device_id_type=MESH)
+        for k in range(NCH // 2):
+            firsts[k].wait_send()
+
+        @pl.when(zl == 0)
+        def _():
+            for q in range(MIDDLE, ZL):
+                pl.semaphore_signal(token.at[1], inc=1, device_id=at(zl=q), device_id_type=MESH)
+        for k in range(NCH // 2, NCH):
+            firsts[k].wait_send()
+
+        @pl.when(zl <= MIDDLE)
+        def _():
+            pl.semaphore_wait(token.at[0], 1)
+
+        @pl.when(zl > MIDDLE)
+        def _():
+            pl.semaphore_wait(token.at[1], 1)
+    for k in range(NCH):
+        send_chunk(y, 0, k, second, top)
 
     @pl.when(via1 | via3)
     def _():
@@ -443,10 +487,8 @@
                 else:
                     base[rows, :] = base[rows, :] - val
 
-            def tile(i, carry):
+            for i in range(X):
                 blocks(i, uhl, store, at_col)
-                return carry
-            lax.fori_loop(0, X, tile, 0)
 
         line_step(y, False)
         for rel in (1, 3, 2):
@@ -491,12 +533,14 @@
             pltpu.VMEM((128, COLS), F32),
             pltpu.VMEM((KC, COLS), F32),
             pltpu.VMEM((ROWS, 128), BF16),
+            pltpu.VMEM((NB, SLOTS), BF16),
             pltpu.VMEM((ROWS, COLS), F32),
             pltpu.VMEM((4, ROWS // 2, COLS), F32),
             pltpu.VMEM((QR, 2 * COLS), BF16),
             pltpu.SemaphoreType.DMA((192,)),
             pltpu.SemaphoreType.DMA((64,)),
             pltpu.SemaphoreType.DMA((3,)),
+            pltpu.SemaphoreType.REGULAR((2,)),
         ],
         compiler_params=pltpu.CompilerParams(
             collective_id=0, has_side_effects=True, vmem_limit_bytes=40 * 2**20

time: 75 us -> 76.6 us (1.021)
  the two profiles are of different devices: /device:TPU:640 before, /device:TPU:256 now
where the time goes in v3:
time: 76.6 us; the launch traced here: 76.3 us
  Pallas kernels  73.2 us (96%)
  local copies, waits for them, and re-layouts  3.1 us (4%)
    pallas_call x1, Pallas kernels, per_device(): pl.pallas_call(kernel, out_shape=jax.ShapeDtypeStruct((ROWS, COLS), F32),...  73.2 us
    unnamed x7, local copies, waits for them, and re-layouts  3.1 us

profile of v3, /device:TPU:256, one launch (start us, length us, event | category | flops | bytes accessed | tf_op | source)
XLA Modules:
  0.0 76.3 jit_solution(4836243910204117351)
XLA Ops:
  0.0 0.0 copy-start
  0.0 0.9 %copy-done = f32[512,128]{1,0:T(8,128)S(1)} copy-done((f32[512,128]{1,0:T(8,128)S(1)}, f32[512,128]{1,0:T(8,128)}, u32[]{:S(2)}) %copy-start) | copy-done | bytes 262168
  1.0 0.0 copy-start.1
  1.0 0.8 copy-done.1
  1.7 0.0 copy-start.2
  1.7 0.7 copy-done.2
  2.4 73.2 %shard_map.37 = f32[512,128]{1,0:T(8,128)S(1)} custom-call(f32[512,128]{1,0:T(8,128)S(1)} %copy-done, f32[8,1024]{1,0:T(8,128)S(1)} %copy-done.1, s32[1,1024]{1,0:T(1,128)S(1)} %bitcast.1), custom_call_target="tpu_custom_call" | custom-call | tf_op jit(solution)/shard_map/pallas_call | solution.py:512
  75.6 0.7 copy.5
Async XLA Ops:
  0.0 0.9 %copy-start = (f32[512,128]{1,0:T(8,128)S(1)}, f32[512,128]{1,0:T(8,128)}, u32[]{:S(2)}) copy-start(f32[512,128]{1,0:T(8,128)} %mat_hbm.1) | copy-start | bytes 786436
  1.0 0.8 copy-start.1
  1.7 0.7 copy-start.2

commit v4 on v3

--- a/solution.py
+++ b/solution.py
@@ -19,8 +19,6 @@
 BITS = ZL.bit_length() - 1
 HALF = ZL // 2
 QR = NB // 4
-MIDDLE = 4
-UPS = 5
 
 
 def rev(s):
@@ -103,10 +101,10 @@
     root = top & (y < 2)
     notroot = (zh > 0) | (y >= 2)
     inner = (zh == 1) | (zh == 3)
-    high = zl // UPS
-    first = at(zh=3 - 2 * high)
-    second = at(zh=1 + 2 * high)
-    via1, via3 = (zh == 1) & (high == 1), (zh == 3) & (high == 0)
+    low = zl // (ZL // 2)
+    first = at(zh=3 - 2 * low)
+    second = at(zh=1 + 2 * low)
+    via1, via3 = (zh == 1) & (low == 1), (zh == 3) & (low == 0)
 
     barrier = pltpu.get_barrier_semaphore()
 
@@ -394,7 +392,7 @@
                 send_chunk(3, 0, k, ydev[3], r0)
                 send_chunk(2, 0, k, ydev[1], r1)
             else:
-                send_first(k, root & (zl != MIDDLE))
+                send_first(k, root)
     for k in range(NCH):
         send_chunk(3, 1, k, ydev[2], r0)
         send_chunk(0, 2, k, ydev[2], r0)
@@ -408,37 +406,14 @@
         @pl.when(nonroot)
         def _():
             arrived(chunk(y, k), ukey(0, k))
-        send_first(k, nonroot & (zl != MIDDLE))
-
-    @pl.when(top & (zl == MIDDLE))
-    def _():
-        pl.semaphore_wait(token.at[1], 1)
+        send_first(k, nonroot)
+
+    @pl.when(top)
+    def _():
         for cp in firsts:
-            cp.start()
-
-    @pl.when(top)
-    def _():
-        @pl.when(zl == ZL - 1)
-        def _():
-            for q in range(MIDDLE, -1, -1):
-                pl.semaphore_signal(token.at[0], inc=1, device_id=at(zl=q), device_id_type=MESH)
-        for k in range(NCH // 2):
-            firsts[k].wait_send()
-
-        @pl.when(zl == 0)
-        def _():
-            for q in range(MIDDLE, ZL):
-                pl.semaphore_signal(token.at[1], inc=1, device_id=at(zl=q), device_id_type=MESH)
-        for k in range(NCH // 2, NCH):
-            firsts[k].wait_send()
-
-        @pl.when(zl <= MIDDLE)
-        def _():
-            pl.semaphore_wait(token.at[0], 1)
-
-        @pl.when(zl > MIDDLE)
-        def _():
-            pl.semaphore_wait(token.at[1], 1)
+            cp.wait_send()
+        pl.semaphore_signal(token, inc=1, device_id=zdev[BITS - 1], device_id_type=MESH)
+        pl.semaphore_wait(token, 1)
     for k in range(NCH):
         send_chunk(y, 0, k, second, top)
 
@@ -540,7 +515,7 @@
             pltpu.SemaphoreType.DMA((192,)),
             pltpu.SemaphoreType.DMA((64,)),
             pltpu.SemaphoreType.DMA((3,)),
-            pltpu.SemaphoreType.REGULAR((2,)),
+            pltpu.SemaphoreType.REGULAR,
         ],
         compiler_params=pltpu.CompilerParams(
             collective_id=0, has_side_effects=True, vmem_limit_bytes=40 * 2**20

time: 76.6 us -> 73.1 us (0.954)
  the two profiles are of different devices: /device:TPU:256 before, /device:TPU:354 now
where the time goes in v4:
time: 73.1 us; the launch traced here: 72.9 us
  Pallas kernels  69.8 us (95%)
  local copies, waits for them, and re-layouts  3.1 us (4%)
    pallas_call x1, Pallas kernels, per_device(): pl.pallas_call(kernel, out_shape=jax.ShapeDtypeStruct((ROWS, COLS), F32),...  69.8 us
    unnamed x7, local copies, waits for them, and re-layouts  3.1 us

profile of v4, /device:TPU:354, one launch (start us, length us, event | category | flops | bytes accessed | tf_op | source)
XLA Modules:
  0.0 72.9 jit_solution(14985687300474112479)
XLA Ops:
  0.0 0.0 copy-start
  0.0 0.9 %copy-done = f32[512,128]{1,0:T(8,128)S(1)} copy-done((f32[512,128]{1,0:T(8,128)S(1)}, f32[512,128]{1,0:T(8,128)}, u32[]{:S(2)}) %copy-start) | copy-done | bytes 262168
  1.0 0.0 copy-start.1
  1.0 0.8 %copy-done.1 = f32[8,1024]{1,0:T(8,128)S(1)} copy-done((f32[8,1024]{1,0:T(8,128)S(1)}, f32[8,1024]{1,0:T(8,128)}, u32[]{:S(2)}) %copy-start.1) | copy-done | bytes 32792
  1.7 0.0 copy-start.2
  1.7 0.7 copy-done.2
  2.4 69.8 %shard_map.37 = f32[512,128]{1,0:T(8,128)S(1)} custom-call(f32[512,128]{1,0:T(8,128)S(1)} %copy-done, f32[8,1024]{1,0:T(8,128)S(1)} %copy-done.1, s32[1,1024]{1,0:T(1,128)S(1)} %bitcast.1), custom_call_target="tpu_custom_call" | custom-call | tf_op jit(solution)/shard_map/pallas_call | solution.py:487
  72.2 0.7 copy.5
Async XLA Ops:
  0.0 0.9 %copy-start = (f32[512,128]{1,0:T(8,128)S(1)}, f32[512,128]{1,0:T(8,128)}, u32[]{:S(2)}) copy-start(f32[512,128]{1,0:T(8,128)} %mat_hbm.1) | copy-start | bytes 786436
  1.0 0.8 %copy-start.1 = (f32[8,1024]{1,0:T(8,128)S(1)}, f32[8,1024]{1,0:T(8,128)}, u32[]{:S(2)}) copy-start(f32[8,1024]{1,0:T(8,128)} %pan_hbm.1) | copy-start | bytes 98308
  1.7 0.7 copy-start.2

commit v5 on v4

--- a/solution.py
+++ b/solution.py
@@ -412,7 +412,18 @@
     def _():
         for cp in firsts:
             cp.wait_send()
-        pl.semaphore_signal(token, inc=1, device_id=zdev[BITS - 1], device_id_type=MESH)
+
+        @pl.when((zl > 0) & (zl < ZL - 1))
+        def _():
+            pl.semaphore_signal(token, inc=1, device_id=zdev[BITS - 1], device_id_type=MESH)
+
+        @pl.when(zl == 1)
+        def _():
+            pl.semaphore_signal(token, inc=1, device_id=at(zl=ZL // 2), device_id_type=MESH)
+
+        @pl.when(zl == ZL - 2)
+        def _():
+            pl.semaphore_signal(token, inc=1, device_id=at(zl=ZL // 2 - 1), device_id_type=MESH)
         pl.semaphore_wait(token, 1)
     for k in range(NCH):
         send_chunk(y, 0, k, second, top)

time: 73.1 us -> 72.1 us (0.986)
  the two profiles are of different devices: /device:TPU:354 before, /device:TPU:356 now
where the time goes in v5:
time: 72.1 us; the launch traced here: 71.9 us
  Pallas kernels  68.8 us (95%)
  local copies, waits for them, and re-layouts  3.1 us (4%)
    pallas_call x1, Pallas kernels, per_device(): pl.pallas_call(kernel, out_shape=jax.ShapeDtypeStruct((ROWS, COLS), F32),...  68.8 us
    unnamed x7, local copies, waits for them, and re-layouts  3.1 us

profile of v5, /device:TPU:356, one launch (start us, length us, event | category | flops | bytes accessed | tf_op | source)
XLA Modules:
  0.0 71.9 jit_solution(7640888787746255178)
XLA Ops:
  0.0 0.0 copy-start
  0.0 0.9 %copy-done = f32[512,128]{1,0:T(8,128)S(1)} copy-done((f32[512,128]{1,0:T(8,128)S(1)}, f32[512,128]{1,0:T(8,128)}, u32[]{:S(2)}) %copy-start) | copy-done | bytes 262168
  1.0 0.0 copy-start.1
  1.0 0.8 %copy-done.1 = f32[8,1024]{1,0:T(8,128)S(1)} copy-done((f32[8,1024]{1,0:T(8,128)S(1)}, f32[8,1024]{1,0:T(8,128)}, u32[]{:S(2)}) %copy-start.1) | copy-done | bytes 32792
  1.7 0.0 copy-start.2
  1.7 0.7 copy-done.2
  2.4 68.8 %shard_map.37 = f32[512,128]{1,0:T(8,128)S(1)} custom-call(f32[512,128]{1,0:T(8,128)S(1)} %copy-done, f32[8,1024]{1,0:T(8,128)S(1)} %copy-done.1, s32[1,1024]{1,0:T(1,128)S(1)} %bitcast.1), custom_call_target="tpu_custom_call" | custom-call | tf_op jit(solution)/shard_map/pallas_call | solution.py:498
  71.2 0.7 copy.5
Async XLA Ops:
  0.0 0.9 %copy-start = (f32[512,128]{1,0:T(8,128)S(1)}, f32[512,128]{1,0:T(8,128)}, u32[]{:S(2)}) copy-start(f32[512,128]{1,0:T(8,128)} %mat_hbm.1) | copy-start | bytes 786436
  1.0 0.8 %copy-start.1 = (f32[8,1024]{1,0:T(8,128)S(1)}, f32[8,1024]{1,0:T(8,128)}, u32[]{:S(2)}) copy-start(f32[8,1024]{1,0:T(8,128)} %pan_hbm.1) | copy-start | bytes 98308
  1.7 0.7 copy-start.2

commit v6 on v5

--- a/solution.py
+++ b/solution.py
@@ -408,14 +408,13 @@
             arrived(chunk(y, k), ukey(0, k))
         send_first(k, nonroot)
 
-    @pl.when(top)
+    inside = (zl > 0) & (zl < ZL - 1)
+
+    @pl.when(top & inside)
     def _():
         for cp in firsts:
             cp.wait_send()
-
-        @pl.when((zl > 0) & (zl < ZL - 1))
-        def _():
-            pl.semaphore_signal(token, inc=1, device_id=zdev[BITS - 1], device_id_type=MESH)
+        pl.semaphore_signal(token, inc=1, device_id=zdev[BITS - 1], device_id_type=MESH)
 
         @pl.when(zl == 1)
         def _():
@@ -424,9 +423,13 @@
         @pl.when(zl == ZL - 2)
         def _():
             pl.semaphore_signal(token, inc=1, device_id=at(zl=ZL // 2 - 1), device_id_type=MESH)
+
+    @pl.when(top)
+    def _():
         pl.semaphore_wait(token, 1)
     for k in range(NCH):
         send_chunk(y, 0, k, second, top)
+    pending.append((top & ((zl == 0) | (zl == ZL - 1)), firsts))
 
     @pl.when(via1 | via3)
     def _():

time: 72.1 us -> 71.2 us (0.988)
  the two profiles are of different devices: /device:TPU:356 before, /device:TPU:352 now
where the time goes in v6:
time: 71.2 us; the launch traced here: 71 us
  Pallas kernels  67.9 us (95%)
  local copies, waits for them, and re-layouts  3.1 us (4%)
    pallas_call x1, Pallas kernels, per_device(): pl.pallas_call(kernel, out_shape=jax.ShapeDtypeStruct((ROWS, COLS), F32),...  67.9 us
    unnamed x7, local copies, waits for them, and re-layouts  3.1 us

profile of v6, /device:TPU:352, one launch (start us, length us, event | category | flops | bytes accessed | tf_op | source)
XLA Modules:
  0.0 71.0 jit_solution(16519376926468991723)
XLA Ops:
  0.0 0.0 copy-start
  0.0 0.9 %copy-done = f32[512,128]{1,0:T(8,128)S(1)} copy-done((f32[512,128]{1,0:T(8,128)S(1)}, f32[512,128]{1,0:T(8,128)}, u32[]{:S(2)}) %copy-start) | copy-done | bytes 262168
  1.0 0.0 copy-start.1
  1.0 0.8 %copy-done.1 = f32[8,1024]{1,0:T(8,128)S(1)} copy-done((f32[8,1024]{1,0:T(8,128)S(1)}, f32[8,1024]{1,0:T(8,128)}, u32[]{:S(2)}) %copy-start.1) | copy-done | bytes 32792
  1.7 0.0 copy-start.2
  1.7 0.7 copy-done.2
  2.4 67.9 %shard_map.37 = f32[512,128]{1,0:T(8,128)S(1)} custom-call(f32[512,128]{1,0:T(8,128)S(1)} %copy-done, f32[8,1024]{1,0:T(8,128)S(1)} %copy-done.1, s32[1,1024]{1,0:T(1,128)S(1)} %bitcast.1), custom_call_target="tpu_custom_call" | custom-call | tf_op jit(solution)/shard_map/pallas_call | solution.py:501
  70.3 0.7 copy.5
Async XLA Ops:
  0.0 0.9 %copy-start = (f32[512,128]{1,0:T(8,128)S(1)}, f32[512,128]{1,0:T(8,128)}, u32[]{:S(2)}) copy-start(f32[512,128]{1,0:T(8,128)} %mat_hbm.1) | copy-start | bytes 786436
  1.0 0.8 %copy-start.1 = (f32[8,1024]{1,0:T(8,128)S(1)}, f32[8,1024]{1,0:T(8,128)}, u32[]{:S(2)}) copy-start(f32[8,1024]{1,0:T(8,128)} %pan_hbm.1) | copy-start | bytes 98308
  1.7 0.7 copy-start.2

commit v7 on v6

--- a/solution.py
+++ b/solution.py
@@ -313,13 +313,11 @@
             for z in range(ZH):
                 arrived(vall.at[src, z], ("vy", d, z))
 
-        def vsplit(i, carry):
+        for i in range(Y):
             for z in range(ZH):
                 hi, lo = split(vall[i, z])
                 vhl[pl.ds(i * (ZH * KC) + z * KC, KC), 0:128] = hi
                 vhl[pl.ds(i * (ZH * KC) + z * KC, KC), 128:256] = lo
-            return carry
-        lax.fori_loop(0, Y, vsplit, 0)
 
         def form(i, q, line):
             rows = pl.ds(q * QR + i * 128, 128)
@@ -330,10 +328,8 @@
                 stay, thm[rows, :].astype(F32), moved).astype(BF16)
 
         def form_two(q, line):
-            def body(i, carry):
+            for i in range(QR // 128):
                 form(i, q, line)
-                return carry
-            lax.fori_loop(0, 2, body, 0)
 
         form_two(0, NATURAL[0])
         form_two(1, NATURAL[1])

time: 71.2 us -> 70.9 us (level)
  the two profiles are of different devices: /device:TPU:352 before, /device:TPU:354 now
where the time goes in v7:
time: 70.9 us; the launch traced here: 70.4 us
  Pallas kernels  67.3 us (95%)
  local copies, waits for them, and re-layouts  3.1 us (4%)
    pallas_call x1, Pallas kernels, per_device(): pl.pallas_call(kernel, out_shape=jax.ShapeDtypeStruct((ROWS, COLS), F32),...  67.3 us
    unnamed x7, local copies, waits for them, and re-layouts  3.1 us

profile of v7, /device:TPU:354, one launch (start us, length us, event | category | flops | bytes accessed | tf_op | source)
XLA Modules:
  0.0 70.4 jit_solution(3889784792420199894)
XLA Ops:
  0.0 0.0 copy-start
  0.0 0.9 %copy-done = f32[512,128]{1,0:T(8,128)S(1)} copy-done((f32[512,128]{1,0:T(8,128)S(1)}, f32[512,128]{1,0:T(8,128)}, u32[]{:S(2)}) %copy-start) | copy-done | bytes 262168
  1.0 0.0 copy-start.1
  1.0 0.8 %copy-done.1 = f32[8,1024]{1,0:T(8,128)S(1)} copy-done((f32[8,1024]{1,0:T(8,128)S(1)}, f32[8,1024]{1,0:T(8,128)}, u32[]{:S(2)}) %copy-start.1) | copy-done | bytes 32792
  1.7 0.0 copy-start.2
  1.7 0.7 copy-done.2
  2.4 67.3 %shard_map.37 = f32[512,128]{1,0:T(8,128)S(1)} custom-call(f32[512,128]{1,0:T(8,128)S(1)} %copy-done, f32[8,1024]{1,0:T(8,128)S(1)} %copy-done.1, s32[1,1024]{1,0:T(1,128)S(1)} %bitcast.1), custom_call_target="tpu_custom_call" | custom-call | tf_op jit(solution)/shard_map/pallas_call | solution.py:497
  69.7 0.7 %copy.5 = f32[512,128]{1,0:T(8,128)} copy(f32[512,128]{1,0:T(8,128)S(1)} %shard_map.37) | data formatting | bytes 524288
Async XLA Ops:
  0.0 0.9 %copy-start = (f32[512,128]{1,0:T(8,128)S(1)}, f32[512,128]{1,0:T(8,128)}, u32[]{:S(2)}) copy-start(f32[512,128]{1,0:T(8,128)} %mat_hbm.1) | copy-start | bytes 786436
  1.0 0.8 %copy-start.1 = (f32[8,1024]{1,0:T(8,128)S(1)}, f32[8,1024]{1,0:T(8,128)}, u32[]{:S(2)}) copy-start(f32[8,1024]{1,0:T(8,128)} %pan_hbm.1) | copy-start | bytes 98308
  1.7 0.7 copy-start.2
